TPU v7x, 32 devices: a whole 2x2x4 slice. The times are simulated.
32 devices in a mesh: pole: 2 (over y), prow: 1, pcol: 16 (over z, x, core).
Axes of the slice: x: 2, y: 2, z: 4, core: 2. Of those that a mesh axis runs over, the one named last changes fastest.
Arguments:
- anc_inverse: float32 [12288, 6144], P(('pole', 'prow'), 'pcol'), parts along dimension 0, may hold values from -8 to 8
- anc_factor: float32 [12288, 768], P(('pole', 'pcol')), parts along dimension 0, may hold values from -0.078125 to 0.078125
- win_factor: float32 [1536, 768], P('pole'), parts along dimension 0, may hold values from -0.375 to 0.375
- pivot_inverse: float32 [6, 256, 256], P('pole'), parts along dimension 0, may hold values from -6 to 6
- structure: int32 [3, 24], replicated, may hold values 0 or 1
Outputs:
- anc_columns: float32 [12288, 768], P(('pole', 'prow', 'pcol')), parts along dimension 0
- win_inverse: float32 [1536, 768], P('pole'), parts along dimension 0
There are 2 independent parts, one for each index of `pole`. A program takes and returns all parts, laid end to end along the dimension named above; an argument that names none is the same for every part. Nothing has to cross between parts.
All inputs are finite; a program needn't handle non-finite values.
Results may differ from a plain program's by a relative error of at most 0.0001.
Values sent between devices are 32-bit elements; how exact they have to be, the bound alone decides.
A program may use at most 128 MiB of HBM per device.

v0:
```python
import jax
import jax.numpy as jnp
from jax import lax
from jax.sharding import PartitionSpec as P

precise = lax.Precision.HIGHEST


def product(left, right):
    return jnp.dot(left, right, precision=precise, preferred_element_type=jnp.float32)


def on_device(anc_inverse, anc_factor, win_factor, pivot_inverse, structure):
    row_count = lax.axis_size("prow")
    col_count = lax.axis_size("pcol")
    row_index = lax.axis_index("prow")
    col_index = lax.axis_index("pcol")
    block_rows = anc_inverse.shape[0]
    block_cols = anc_inverse.shape[1]
    steps_total = pivot_inverse.shape[0]
    width = pivot_inverse.shape[1]
    all_cols = anc_factor.shape[1]
    block_count = structure.shape[1]
    ratio_cols = col_count // row_count
    share_rows = block_rows // col_count
    structure_cols = structure.T.astype(jnp.float32)
    global_rows = col_index * block_cols + lax.iota(jnp.int32, block_cols)
    onehot_rows = (
        (global_rows // width)[:, None] == lax.iota(jnp.int32, block_count)[None, :]
    ).astype(jnp.float32)
    kept_rows = product(onehot_rows, structure_cols)
    share_offset = col_index * share_rows
    share_global = (row_index * col_count + col_index) * share_rows + lax.iota(
        jnp.int32, share_rows
    )
    onehot_share = (
        (share_global // width)[:, None] == lax.iota(jnp.int32, block_count)[None, :]
    ).astype(jnp.float32)
    kept_share = product(onehot_share, structure_cols)
    slot_ids = lax.iota(jnp.int32, col_count)
    source_flag = (slot_ids // row_count == col_index - row_index * ratio_cols).astype(jnp.float32)
    pieces = jnp.tile(anc_factor.reshape(row_count, share_rows, all_cols), (ratio_cols, 1, 1))
    outgoing = pieces * source_flag[:, None, None]
    incoming = lax.all_to_all(outgoing, "pcol", split_axis=0, concat_axis=0, tiled=True)
    factor_share = jnp.sum(incoming, axis=0)
    column_store = {}
    share_store = {}
    window_blocks = {}
    for k in range(steps_total - 1, -1, -1):
        first_col = k * width
        factor_now = anc_factor[:, first_col : first_col + width] * kept_rows[:, k : k + 1]
        share_factor = factor_share[:, first_col : first_col + width] * kept_share[:, k : k + 1]
        finished = list(range(k + 1, steps_total))
        if finished:
            stacked = jnp.concatenate([column_store[j] for j in finished], axis=1)
            factor_win = win_factor[first_col + width :, first_col : first_col + width]

        def term_rows(start, count, factor_now=factor_now):
            return product(anc_inverse, factor_now)

        share_image = lax.psum_scatter(
            term_rows(jnp.int32(0), share_rows * lax.axis_size("pcol")),
            "pcol",
            scatter_dimension=0,
            tiled=True,
        )
        if finished:
            share_image = share_image + product(
                lax.dynamic_slice_in_dim(stacked, share_offset, share_rows, 0), factor_win
            )
        share_column = -share_image
        column_now = lax.all_gather(share_column, "pcol", axis=0, tiled=True)
        crossings = [product(share_store[j].T, share_factor) for j in finished]
        pivot_part = product(share_factor.T, share_column)
        cross_sums = []
        if finished:
            cross_total = lax.psum(jnp.stack(crossings), ("prow", "pcol"))
            cross_sums = [cross_total[position] for position in range(len(finished))]
        pivot_sum = lax.psum(pivot_part, ("prow", "pcol"))
        for position, j in enumerate(finished):
            running = cross_sums[position]
            for i in finished:
                running = running + product(
                    window_blocks[j, i],
                    win_factor[i * width : (i + 1) * width, first_col : first_col + width],
                )
            window_blocks[j, k] = -running
            window_blocks[k, j] = -running.T
        pivot_block = pivot_inverse[k] - pivot_sum
        for j in finished:
            pivot_block = pivot_block - product(
                win_factor[j * width : (j + 1) * width, first_col : first_col + width].T,
                window_blocks[j, k],
            )
        window_blocks[k, k] = pivot_block
        column_store[k] = column_now
        share_store[k] = share_column
    anc_columns = jnp.concatenate([share_store[k] for k in range(steps_total)], axis=1)
    win_inverse = jnp.concatenate(
        [
            jnp.concatenate([window_blocks[i, k] for k in range(steps_total)], axis=1)
            for i in range(steps_total)
        ],
        axis=0,
    )
    return (anc_columns, win_inverse)


def solution(mesh):
    in_specs = (
        P(("pole", "prow"), "pcol"),
        P(("pole", "pcol"), None),
        P("pole", None),
        P("pole", None, None),
        P(),
    )
    out_specs = (P(("pole", "prow", "pcol"), None), P("pole", None))
    return jax.shard_map(
        on_device, mesh=mesh, in_specs=in_specs, out_specs=out_specs, check_vma=False
    )
```

profile of v0, /device:TPU:0, one launch (start us, length us, event | category | flops | bytes accessed | tf_op | source)
XLA Modules:
  0.0 905.3 jit_solution(14524148858973868540)
XLA Ops:
  7.2 0.0 reduce-scatter.8.cloned.1.call-start
  7.2 1.0 fusion.40
  8.2 19.4 %convolution_bitcast_fusion = f32[6144,256]{0,1:T(8,128)} fusion(f32[6144,384]{1,0:T(8,128)} %param.5, f32[384,768]{1,0:T(8,128)} %param.6, f32[384]{0:T(512)S(1)} %get-tuple-element.7), kind=kOutput, calls=%fused_computation.3 | convolution fusion | flops 7247855616 | bytes 16123392 | tf_op jit(solution)/shard_map/dot_general | solution.py:10
  27.6 0.0 reduce-scatter.8.cloned.1.call-update
  27.6 0.2 reduce-scatter.6.cloned.1.call-start
  27.9 1.0 copy-done.2
  28.9 19.2 %convolution_bitcast_fusion.1 = f32[6144,256]{0,1:T(8,128)} fusion(f32[6144,384]{1,0:T(8,128)} %param.5, f32[384,768]{1,0:T(8,128)S(1)} %copy-done.2, f32[384]{0:T(512)S(1)} %get-tuple-element.8), kind=kOutput, calls=%fused_computation.4 | convolution fusion | flops 7247855616 | bytes 16123904 | tf_op jit(solution)/shard_map/dot_general | solution.py:10
  48.1 0.0 reduce-scatter.6.cloned.1.call-update
  48.1 8.4 broadcast_multiply_fusion
  56.5 7.4 all-to-all-start
  63.9 0.0 all-gather.3.cloned.1.call-start
  63.9 346.9 %reduce-scatter.8.cloned.1.call-done = f32[384,256]{0,1:T(8,128)} async-done(((f32[6144,256]{0,1:T(8,128)}), f32[384,256]{0,1:T(8,128)}) %reduce-scatter.8.cloned.1.call-update) | async-done | bytes 393232 | tf_op jit(solution)/shard_map/reduce_scatter | solution.py:61
  410.8 1.8 neg.30
  412.6 0.0 all-gather.3.cloned.1.call-update
  412.6 0.3 reduce-scatter.4.cloned.1.call-start
  412.9 19.2 %convolution_bitcast_fusion.2 = f32[6144,256]{0,1:T(8,128)} fusion(f32[6144,384]{1,0:T(8,128)} %param.5, f32[384,768]{1,0:T(8,128)S(1)} %copy-done.2, f32[384]{0:T(512)S(1)} %get-tuple-element.6), kind=kOutput, calls=%fused_computation.5 | convolution fusion | flops 7247855616 | bytes 16123904 | tf_op jit(solution)/shard_map/dot_general | solution.py:10
  432.1 0.0 reduce-scatter.4.cloned.1.call-update
  432.1 0.0 all-gather.5.cloned.1.call-start
  432.2 121.9 %reduce-scatter.6.cloned.1.call-done = f32[384,256]{0,1:T(8,128)} async-done(((f32[6144,256]{0,1:T(8,128)}), f32[384,256]{0,1:T(8,128)}) %reduce-scatter.6.cloned.1.call-update) | async-done | bytes 393232 | tf_op jit(solution)/shard_map/reduce_scatter | solution.py:61
  554.1 64.0 %all-gather.3.cloned.1.call-done = f32[6144,256]{0,1:T(8,128)} async-done(((f32[384,256]{0,1:T(8,128)}), f32[6144,256]{0,1:T(8,128)}) %all-gather.3.cloned.1.call-update) | async-done | bytes 6291472 | tf_op jit(solution)/shard_map/all_gather | solution.py:72
  618.1 2.6 fusion.1
  620.7 0.0 all-gather.5.cloned.1.call-update
  620.7 0.3 all-reduce.3.cloned.1.call-start
  621.0 84.6 %reduce-scatter.4.cloned.1.call-done = f32[384,256]{0,1:T(8,128)} async-done(((f32[6144,256]{0,1:T(8,128)}), f32[384,256]{0,1:T(8,128)}) %reduce-scatter.4.cloned.1.call-update) | async-done | bytes 393232 | tf_op jit(solution)/shard_map/reduce_scatter | solution.py:61
  705.7 64.0 %all-gather.5.cloned.1.call-done = f32[6144,256]{0,1:T(8,128)} async-done(((f32[384,256]{0,1:T(8,128)}), f32[6144,256]{0,1:T(8,128)}) %all-gather.5.cloned.1.call-update) | async-done | bytes 6291472 | tf_op jit(solution)/shard_map/all_gather | solution.py:72
  769.7 2.4 fusion
  772.1 0.0 copy-start
  772.1 0.0 all-to-all-done
  772.1 7.7 reduce_sum.9
  779.8 0.0 copy-done
  779.8 0.0 copy-start.1
  779.8 0.9 convolution_bitcast_fusion.7
  780.7 1.4 fusion.20
  782.1 1.6 fusion.21
  783.7 0.0 copy-done.1
  783.7 0.9 convolution_bitcast_fusion.6
  784.6 0.8 pad_maximum_fusion.2
  785.4 1.4 fusion.19
  786.8 1.6 fusion.11
  788.3 0.0 all-reduce.3.cloned.1.call-update
  788.4 0.0 slice-done
  788.4 0.8 copy.42
  789.2 0.0 copy-done.3
  789.2 0.1 pad_maximum_fusion
  789.3 1.4 copy.32
  790.7 93.1 %all-reduce.3.cloned.1.call-done = (f32[256,256]{1,0:T(8,128)}, f32[256,256]{1,0:T(8,128)}, f32[2,256,256]{1,2,0:T(8,128)}, f32[256,256]{0,1:T(8,128)}, f32[256,256]{1,0:T(8,128)}) async-done(((f32[256,256]{1,0:T(8,128)}, f32[256,256]{1,0:T(8,128)}, f32[2,256,256]{1,2,0:T(8,128)}, f32[256,256]{0,1:T(8,128)}, f32[256,256]{1,0:T(8,128)}), (f32[256,256]{1,0:T(8,128)}, f32[256,256]{1,0:T(8,128)}, ...) | async-done | bytes 1572880 | tf_op jit(solution)/shard_map/psum | solution.py:79
  883.8 1.1 bitcast_subtract_fusion
  884.9 1.4 fusion.7
  886.3 1.6 convolution_add_fusion.3
  887.9 0.0 copy-done.4
  888.0 1.5 fusion.6
  889.5 0.7 copy-done.5
  890.2 0.0 copy-done.10
  890.2 0.6 convolution_add_fusion.5
  890.8 0.6 fusion.5
  891.4 0.6 fusion.3
  892.0 0.8 copy.30
  892.9 1.7 fusion.4
  894.6 1.3 fusion.2
  895.9 0.1 pad_maximum_fusion.1
  895.9 0.3 copy.31
  896.2 0.6 copy-done.8
  896.8 0.1 copy-done.9
  896.9 1.6 maximum_maximum_fusion
  (15 shorter events, 0.1 us)
Async XLA Ops:
  7.2 403.7 %reduce-scatter.8.cloned.1.call-start = ((), (), s32[]{:S(2)}) async-start(), calls=%async_computation.6 | async-start | bytes 6684672 | tf_op jit(solution)/shard_map/reduce_scatter | solution.py:61
  27.6 1.3 copy-start.2
  27.6 526.5 %reduce-scatter.6.cloned.1.call-start = ((), (), s32[]{:S(2)}) async-start(), calls=%async_computation.5 | async-start | bytes 6684672 | tf_op jit(solution)/shard_map/reduce_scatter | solution.py:61
  56.5 715.6 %all-to-all-start = ((f32[16,384,768]{2,1,0:T(8,128)}), f32[16,384,768]{2,1,0:T(8,128)}, u32[]{:S(2)}, u32[]{:S(2)}) async-start(f32[16,384,768]{2,1,0:T(8,128)} %broadcast_multiply_fusion), calls=%async_computation.3 | async-start | bytes 37748736 | tf_op jit(solution)/shard_map/all_to_all | solution.py:44
  63.9 554.3 %all-gather.3.cloned.1.call-start = ((), (), s32[]{:S(2)}) async-start(), calls=%async_computation.7 | async-start | bytes 6684672 | tf_op jit(solution)/shard_map/all_gather | solution.py:72
  412.6 293.1 %reduce-scatter.4.cloned.1.call-start = ((), (), s32[]{:S(2)}) async-start(), calls=%async_computation.4 | async-start | bytes 6684672 | tf_op jit(solution)/shard_map/reduce_scatter | solution.py:61
  432.1 337.5 %all-gather.5.cloned.1.call-start = ((), (), s32[]{:S(2)}) async-start(), calls=%async_computation.8 | async-start | bytes 6684672 | tf_op jit(solution)/shard_map/all_gather | solution.py:72
  620.7 263.0 %all-reduce.3.cloned.1.call-start = ((), (), s32[]{:S(2)}) async-start(), calls=%async_computation.9 | async-start | bytes 3145728 | tf_op jit(solution)/shard_map/psum | solution.py:79
  772.1 7.7 copy-start
  779.8 3.9 copy-start.1
  785.4 3.0 slice-start
  785.4 3.8 copy-start.3
  790.7 97.3 %copy-start.4 = (f32[768,768]{1,0:T(8,128)S(1)}, f32[768,768]{1,0:T(8,128)}, u32[]{:S(2)}) copy-start(f32[768,768]{1,0:T(8,128)} %param.7) | copy-start | bytes 7077892
  790.7 97.3 %copy-start.7 = (f32[1,256,256]{1,2,0:T(8,128)S(1)}, f32[1,256,256]{1,2,0:T(8,128)}, u32[]{:S(2)}) copy-start(f32[1,256,256]{1,2,0:T(8,128)} %copy.42) | copy-start | bytes 786436
  883.8 6.5 copy-start.10
  889.5 0.7 copy-start.5
  892.9 3.0 copy-start.6
  895.9 0.9 copy-start.8
  895.9 1.0 copy-start.9
Sparse Core Ops, SparseCore 0:
  27.8 383.0 reduce-scatter.7
  415.3 138.7 reduce-scatter.5
  557.0 61.1 all-gather.2
  621.9 83.6 reduce-scatter.3
  708.7 60.9 all-gather.4
  788.5 95.2 all-reduce.2
where the time goes:
time: 906 us; the launch traced here: 905 us
  waiting for transfers between devices  775 us (86%)
  matrix products  80.8 us (9%)
  other arithmetic  21.5 us (2%)
  between operations  14.3 us (2%)
    reduce_scatter x3, waiting for transfers between devices, on_device(): lax.psum_scatter(term_rows(jnp.int32(0), share_rows * lax.axis_size('pcol...  553 us
    all_gather x2, waiting for transfers between devices, on_device(): column_now = lax.all_gather(share_column, 'pcol', axis=0, tiled=True)  128 us
    psum x1, waiting for transfers between devices, on_device(): pivot_sum = lax.psum(pivot_part, ('prow', 'pcol'))  93.1 us
    dot_general x20, matrix products, product(): jnp.dot(left, right, precision=precise, preferred_element_type=jnp.float32)  80.8 us
  transfers between devices with their start and end apart: 7, of which 6 were waited for; matrix products, arithmetic and copies ran while one was open for 6% of the time, Pallas kernels for 0%

commit v1 on v0

--- a/solution.py
+++ b/solution.py
@@ -76,7 +76,7 @@
         if finished:
             cross_total = lax.psum(jnp.stack(crossings), ("prow", "pcol"))
             cross_sums = [cross_total[position] for position in range(len(finished))]
-        pivot_sum = lax.psum(pivot_part, ("prow", "pcol"))
+        pivot_sum = jnp.sum(lax.all_gather(pivot_part, ("prow", "pcol")), axis=0)
         for position, j in enumerate(finished):
             running = cross_sums[position]
             for i in finished:

time: 906 us -> 1040 us (1.15)
  waiting for transfers between devices: 775 us -> 894 us
    all_gather x0 -> x3, waiting for transfers between devices: none -> 137 us  [on_device(): pivot_sum = jnp.sum(lax.all_gather(pivot_part, ('prow', 'pcol')), axis=0)]
    reduce_scatter x3, waiting for transfers between devices: 553 us -> 538 us  [on_device(): lax.psum_scatter(term_rows(jnp.int32(0), share_rows * lax.axis_size('pcol...]
  transfers between devices with their start and end apart: 7 -> 10, of which waited for: 6 -> 9; matrix products, arithmetic and copies ran while one was open for 6% -> 8% of each run, Pallas kernels for 0% -> 0%
where the time goes in v1:
time: 1040 us; the launch traced here: 1030 us
  waiting for transfers between devices  894 us (86%)
  matrix products  79.7 us (8%)
  other arithmetic  30.6 us (3%)
  between operations  14.1 us (1%)
    reduce_scatter x3, waiting for transfers between devices, on_device(): lax.psum_scatter(term_rows(jnp.int32(0), share_rows * lax.axis_size('pcol...  538 us
    all_gather x3, waiting for transfers between devices, on_device(): pivot_sum = jnp.sum(lax.all_gather(pivot_part, ('prow', 'pcol')), axis=0)  137 us
    all_gather x2, waiting for transfers between devices, on_device(): column_now = lax.all_gather(share_column, 'pcol', axis=0, tiled=True)  127 us
    psum x1, waiting for transfers between devices, on_device(): cross_total = lax.psum(jnp.stack(crossings), ('prow', 'pcol'))  91.6 us
    dot_general x20, matrix products, product(): jnp.dot(left, right, precision=precise, preferred_element_type=jnp.float32)  79.7 us
  transfers between devices with their start and end apart: 10, of which 9 were waited for; matrix products, arithmetic and copies ran while one was open for 8% of the time, Pallas kernels for 0%

profile of v1, /device:TPU:0, one launch (start us, length us, event | category | flops | bytes accessed | tf_op | source)
XLA Modules:
  0.0 1034.8 jit_solution(10793104647366736843)
XLA Ops:
  7.2 0.0 reduce-scatter.8.cloned.1.call-start
  7.2 1.0 fusion.40
  8.2 19.4 %convolution_bitcast_fusion = f32[6144,256]{0,1:T(8,128)} fusion(f32[6144,384]{1,0:T(8,128)} %param.5, f32[384,768]{1,0:T(8,128)} %param.6, f32[384]{0:T(512)S(1)} %get-tuple-element.9), kind=kOutput, calls=%fused_computation.3 | convolution fusion | flops 7247855616 | bytes 16123392 | tf_op jit(solution)/shard_map/dot_general | solution.py:10
  27.6 0.0 reduce-scatter.8.cloned.1.call-update
  27.7 0.2 reduce-scatter.6.cloned.1.call-start
  27.9 1.0 copy-done.2
  28.9 19.3 %convolution_bitcast_fusion.1 = f32[6144,256]{0,1:T(8,128)} fusion(f32[6144,384]{1,0:T(8,128)} %param.5, f32[384,768]{1,0:T(8,128)S(1)} %copy-done.2, f32[384]{0:T(512)S(1)} %get-tuple-element.10), kind=kOutput, calls=%fused_computation.4 | convolution fusion | flops 7247855616 | bytes 16123904 | tf_op jit(solution)/shard_map/dot_general | solution.py:10
  48.2 8.4 broadcast_multiply_fusion
  56.6 7.4 all-to-all-start
  64.0 0.0 all-gather.9.cloned.1.call-start
  64.0 346.8 %reduce-scatter.8.cloned.1.call-done = f32[384,256]{0,1:T(8,128)} async-done(((f32[6144,256]{0,1:T(8,128)}), f32[384,256]{0,1:T(8,128)}) %reduce-scatter.8.cloned.1.call-update) | async-done | bytes 393232 | tf_op jit(solution)/shard_map/reduce_scatter | solution.py:61
  410.8 1.8 neg.30
  412.6 0.3 reduce-scatter.4.cloned.1.call-start
  412.9 19.3 %convolution_bitcast_fusion.2 = f32[6144,256]{0,1:T(8,128)} fusion(f32[6144,384]{1,0:T(8,128)} %param.5, f32[384,768]{1,0:T(8,128)S(1)} %copy-done.2, f32[384]{0:T(512)S(1)} %get-tuple-element.8), kind=kOutput, calls=%fused_computation.5 | convolution fusion | flops 7247855616 | bytes 16123904 | tf_op jit(solution)/shard_map/dot_general | solution.py:10
  432.1 0.0 reduce-scatter.4.cloned.1.call-update
  432.2 0.0 all-gather.11.cloned.1.call-start
  432.2 121.9 %reduce-scatter.6.cloned.1.call-done = f32[384,256]{0,1:T(8,128)} async-done(((f32[6144,256]{0,1:T(8,128)}), f32[384,256]{0,1:T(8,128)}) %reduce-scatter.6.cloned.1.call-update) | async-done | bytes 393232 | tf_op jit(solution)/shard_map/reduce_scatter | solution.py:61
  554.1 63.9 %all-gather.9.cloned.1.call-done = f32[6144,256]{0,1:T(8,128)} async-done(((f32[384,256]{0,1:T(8,128)}), f32[6144,256]{0,1:T(8,128)}) %all-gather.9.cloned.1.call-update) | async-done | bytes 6291472 | tf_op jit(solution)/shard_map/all_gather | solution.py:72
  618.0 2.6 fusion.1
  620.6 0.0 all-gather.11.cloned.1.call-update
  620.6 0.0 all-gather.17.cloned.1.call-start
  620.7 8.0 reduce_sum.36
  628.7 1.6 fusion.11
  630.3 0.0 all-gather.17.cloned.1.call-update
  630.3 0.0 all-reduce.3.cloned.1.call-start
  630.4 0.7 convolution_bitcast_fusion.7
  631.0 0.7 convolution_bitcast_fusion.6
  631.7 0.8 pad_maximum_fusion.2
  632.5 1.6 fusion.19
  634.1 0.0 all-reduce.3.cloned.1.call-update
  634.2 0.0 all-gather.15.cloned.1.call-start
  634.2 1.6 fusion.20
  635.8 0.3 all-gather.13.cloned.1.call-start
  636.1 69.4 %reduce-scatter.4.cloned.1.call-done = f32[384,256]{0,1:T(8,128)} async-done(((f32[6144,256]{0,1:T(8,128)}), f32[384,256]{0,1:T(8,128)}) %reduce-scatter.4.cloned.1.call-update) | async-done | bytes 393232 | tf_op jit(solution)/shard_map/reduce_scatter | solution.py:61
  705.5 63.4 %all-gather.11.cloned.1.call-done = f32[6144,256]{0,1:T(8,128)} async-done(((f32[384,256]{0,1:T(8,128)}), f32[6144,256]{0,1:T(8,128)}) %all-gather.11.cloned.1.call-update) | async-done | bytes 6291472 | tf_op jit(solution)/shard_map/all_gather | solution.py:72
  768.9 2.4 fusion
  771.4 1.6 fusion.21
  773.0 0.9 copy.33
  773.9 0.1 pad_maximum_fusion
  774.0 1.4 copy.29
  775.3 44.9 %all-gather.17.cloned.1.call-done = f32[4096,256]{1,0:T(8,128)} async-done(((f32[256,256]{1,0:T(8,128)}), f32[4096,256]{1,0:T(8,128)}) %all-gather.17.cloned.1.call-update) | async-done | bytes 4194320 | tf_op jit(solution)/shard_map/all_gather | solution.py:79
  820.3 2.6 reduce_sum.39
  822.9 1.0 bitcast_subtract_fusion
  823.9 91.6 %all-reduce.3.cloned.1.call-done = (f32[256,256]{0,1:T(8,128)}, f32[2,256,256]{2,1,0:T(8,128)}) async-done(((f32[256,256]{0,1:T(8,128)}, f32[2,256,256]{2,1,0:T(8,128)}), (f32[256,256]{0,1:T(8,128)}, f32[2,256,256]{2,1,0:T(8,128)})) %all-reduce.3.cloned.1.call-update) | async-done | bytes 786448 | tf_op jit(solution)/shard_map/psum | solution.py:77
  915.5 1.5 fusion.7
  917.1 0.8 copy.27
  917.9 49.3 %all-gather.15.cloned.1.call-done = f32[4096,256]{1,0:T(8,128)} async-done(((f32[256,256]{1,0:T(8,128)}), f32[4096,256]{1,0:T(8,128)}) %all-gather.15.cloned.1.call-update) | async-done | bytes 4194320 | tf_op jit(solution)/shard_map/all_gather | solution.py:79
  967.2 3.2 reduce_sum.38
  970.4 1.6 convolution_add_fusion.3
  972.0 0.4 fusion.3
  972.4 1.6 fusion.6
  974.1 0.7 copy-done.5
  974.8 0.4 convolution_add_fusion.5
  975.2 0.4 fusion.5
  975.6 42.9 %all-gather.13.cloned.1.call-done = f32[4096,256]{1,0:T(8,128)} async-done(((f32[256,256]{1,0:T(8,128)}), f32[4096,256]{1,0:T(8,128)}) %all-gather.13.cloned.1.call-update) | async-done | bytes 4194320 | tf_op jit(solution)/shard_map/all_gather | solution.py:79
  1018.5 3.2 reduce_sum.37
  1021.7 1.8 copy.23
  1023.5 1.6 fusion.4
  1025.1 0.6 fusion.2
  1025.7 0.1 pad_maximum_fusion.1
  1025.8 0.3 copy.28
  1026.1 0.6 copy-done.6
  1026.7 0.1 copy-done.7
  1026.7 1.6 maximum_maximum_fusion
  (24 shorter events, 0.2 us)
Async XLA Ops:
  7.2 403.6 %reduce-scatter.8.cloned.1.call-start = ((), (), s32[]{:S(2)}) async-start(), calls=%async_computation.6 | async-start | bytes 6684672 | tf_op jit(solution)/shard_map/reduce_scatter | solution.py:61
  27.6 1.3 copy-start.2
  27.7 526.5 %reduce-scatter.6.cloned.1.call-start = ((), (), s32[]{:S(2)}) async-start(), calls=%async_computation.5 | async-start | bytes 6684672 | tf_op jit(solution)/shard_map/reduce_scatter | solution.py:61
  56.6 564.1 %all-to-all-start = ((f32[16,384,768]{2,1,0:T(8,128)}), f32[16,384,768]{2,1,0:T(8,128)}, u32[]{:S(2)}, u32[]{:S(2)}) async-start(f32[16,384,768]{2,1,0:T(8,128)} %broadcast_multiply_fusion), calls=%async_computation.3 | async-start | bytes 37748736 | tf_op jit(solution)/shard_map/all_to_all | solution.py:44
  64.0 554.0 %all-gather.9.cloned.1.call-start = ((), (), s32[]{:S(2)}) async-start(), calls=%async_computation.7 | async-start | bytes 6684672 | tf_op jit(solution)/shard_map/all_gather | solution.py:72
  412.6 292.9 %reduce-scatter.4.cloned.1.call-start = ((), (), s32[]{:S(2)}) async-start(), calls=%async_computation.4 | async-start | bytes 6684672 | tf_op jit(solution)/shard_map/reduce_scatter | solution.py:61
  432.2 336.8 %all-gather.11.cloned.1.call-start = ((), (), s32[]{:S(2)}) async-start(), calls=%async_computation.8 | async-start | bytes 6684672 | tf_op jit(solution)/shard_map/all_gather | solution.py:72
  620.6 8.1 copy-start.1
  620.6 9.7 copy-start
  620.6 199.6 %all-gather.17.cloned.1.call-start = ((), (), s32[]{:S(2)}) async-start(), calls=%async_computation.11 | async-start | bytes 4456448 | tf_op jit(solution)/shard_map/all_gather | solution.py:79
  630.3 285.2 %all-reduce.3.cloned.1.call-start = ((), (), s32[]{:S(2)}) async-start(), calls=%async_computation.12 | async-start | bytes 1572864 | tf_op jit(solution)/shard_map/psum | solution.py:77
  634.2 333.1 %all-gather.15.cloned.1.call-start = ((), (), s32[]{:S(2)}) async-start(), calls=%async_computation.10 | async-start | bytes 4456448 | tf_op jit(solution)/shard_map/all_gather | solution.py:79
  635.8 137.2 %slice-start = ((f32[3,256,256]{2,1,0:T(8,128)}), f32[1,256,256]{2,1,0:T(8,128)S(1)}, s32[]{:S(2)}) async-start(f32[3,256,256]{2,1,0:T(8,128)} %param.8), calls=%async_computation.13 | async-start | bytes 524288 | tf_op jit(solution)/shard_map/slice | solution.py:89
  635.8 382.7 %all-gather.13.cloned.1.call-start = ((), (), s32[]{:S(2)}) async-start(), calls=%async_computation.9 | async-start | bytes 4456448 | tf_op jit(solution)/shard_map/all_gather | solution.py:79
  771.4 2.5 copy-start.3
  820.3 95.3 %copy-start.4 = (f32[768,768]{1,0:T(8,128)S(1)}, f32[768,768]{1,0:T(8,128)}, u32[]{:S(2)}) copy-start(f32[768,768]{1,0:T(8,128)} %param.7) | copy-start | bytes 7077892
  970.4 4.4 copy-start.8
  974.1 0.7 copy-start.5
  1025.7 1.0 copy-start.6
  1025.7 1.0 copy-start.7
Sparse Core Ops, SparseCore 0:
  27.8 382.9 reduce-scatter.7
  415.3 138.8 reduce-scatter.5
  557.0 60.9 all-gather.8
  621.8 83.6 reduce-scatter.3
  708.0 60.9 all-gather.10
  771.2 49.0 all-gather.16
  824.8 90.7 all-reduce.2
  917.7 49.5 all-gather.14
  969.4 49.0 all-gather.12
